TPU v7x, 128 devices: a whole 4x4x4 slice. The times are simulated.
128 devices in a mesh: prompt: 8 (over z, y_lo), ctx: 16 (over x, y_hi, core).
Axes of the slice: x: 4, y: 4 (y_hi: 2, y_lo: 2; y = y_hi * 2 + y_lo), z: 4, core: 2. Of those that a mesh axis runs over, the one named last changes fastest.
Arguments:
- query_latent: bfloat16 [8, 3072, 1536], P('prompt', 'ctx'), may hold values from -41 to 41
- kv_latent: bfloat16 [8, 3072, 576], P('prompt', 'ctx'), may hold values from -6 to 6
- query_up: bfloat16 [1536, 3072], replicated, may hold values from -0.15625 to 0.15625
- key_absorb: bfloat16 [16, 128, 512], replicated, may hold values from -0.5 to 0.5
- value_up_weight: bfloat16 [16, 512, 128], replicated, may hold values from -0.25 to 0.25
- block_order: int32 [8, 32], P('prompt', 'ctx'), may hold values from 0 to 31, each once within a row
- page_owner: int32 [8, 192, 1], P('prompt', 'ctx'), may hold values from 0 to 7; in each aligned block of 12 rows (0 to 11, 12 to 23, ..., all dimensions but the last counted through in order) at most 3 rows name the same one
Outputs:
- attention_out: bfloat16 [8, 3072, 2048], P('prompt', 'ctx')
- cache_pages: bfloat16 [8, 16, 8, 3, 9216], P('prompt', 'ctx')
- page_start: int32 [8, 16, 8, 3], P('prompt', 'ctx')
Inputs may be any that keep to these rules, and one draw needn't show every extreme that they name: `block_order`: each prompt's row names every block of 96 positions once. `page_owner`: among the 12 pages of one device at most 3 have the same owner.
All inputs are finite; a program needn't handle non-finite values.
Results may differ from a plain program's by a relative error of at most 0.015.
The roundings to bfloat16 on the way count: a program that leaves them out, or rounds other values in their place, can miss the bound.
Values may be sent and summed in bfloat16 or wider, within the bound.
No kernel may reach another device: no remote copies, remote signals or barrier semaphores. Data moves between devices by JAX's collectives and lax.ppermute only.
A program may use at most 128 MiB of HBM per device.

v0:
```python
import functools
import math

import jax
import jax.numpy as jnp
import numpy as np
from jax import lax
from jax.experimental import pallas as pl
from jax.experimental.pallas import tpu as pltpu
from jax.sharding import PartitionSpec as P

F32 = jnp.float32
BF16 = jnp.bfloat16
NOPE, ROPE, KVR, VD, HEADS = 128, 64, 512, 128, 16
LAT = KVR + ROPE
WIDE = 640
PAGE, PAGES, CAP = 16, 12, 3
HALF, ROWS = 96, 192
BLOCKS = 32
FLAT = PAGE * LAT
BIG = 1e30
SCALE2 = (NOPE + ROPE) ** -0.5 * math.log2(math.e)
VMEM_LIMIT = 60 * 2**20
QUERY_VMEM = 60 * 2**20
ATTEND_VMEM = 52 * 2**20
SMALL_VMEM = 8 * 2**20
CHUNK = 512


def rope_tables():
    lane = np.arange(128)
    freq = 10000.0 ** (-2.0 * (lane % 32) / ROPE)
    sign = np.where(lane % 64 < 32, -1.0, 1.0)

    def table(places):
        angle = places[:, None] * freq
        return np.concatenate([np.cos(angle), sign * np.sin(angle)], axis=1).astype(np.float32)

    return table(np.arange(BLOCKS) * float(HALF)), table(np.arange(HALF) * 1.0)


def query_kernel(
    blk_h, ql_h, qu_h, ka_h, tab_h, _, out_h, token, blk, ql, qu, ka, tab, out, rope_s, ext_s, sem
):
    chunks = qu.shape[0]
    width = qu.shape[2]
    copies = [
        pltpu.make_async_copy(blk_h, blk, sem.at[0]),
        pltpu.make_async_copy(tab_h, tab, sem.at[1]),
        pltpu.make_async_copy(ql_h, ql, sem.at[2]),
    ]
    for j in range(chunks):
        part = qu_h.at[:, j * width : (j + 1) * width]
        copies.append(pltpu.make_async_copy(part, qu.at[j], sem.at[4 + j]))
    copies.insert(4, pltpu.make_async_copy(ka_h, ka, sem.at[3]))
    for copy in copies:
        copy.start()
    copies[0].wait()
    copies[1].wait()
    half_lane = lax.broadcasted_iota(jnp.int32, (HALF, 128), 1)
    for slot in range(2):
        here = blk[0, slot]
        base = tab[pl.ds(here, 1), :]
        bc, bs = base[:, :128], base[:, 128:]
        oc, os = tab[BLOCKS:, :128], tab[BLOCKS:, 128:]
        rows = slice(slot * HALF, (slot + 1) * HALF)
        rope_s[rows, :128] = bc * oc - bs * os
        rope_s[rows, 128:] = bs * oc + bc * os
        later = (half_lane >= 64 + here + 1) & (half_lane < 64 + BLOCKS)
        ext_s[rows, :] = jnp.where(later, -BIG, 0.0)
    lane = lax.broadcasted_iota(jnp.int32, (ROWS, 128), 1)
    low = lane < 64
    token[...] = jnp.zeros(token.shape, F32)
    copies[2].wait()
    outgoing = []
    for c in range(chunks):
        copies[3 if c == 0 else 4 + c].wait()
        both = jnp.dot(ql[...], qu[c], preferred_element_type=F32).astype(BF16)
        if c == 0:
            copies[4].wait()
        for j in range(width // 384):
            even, at = (c * width // 384 + j) * 2, 384 * j
            t0 = both[:, at : at + 128]
            t1 = both[:, at + 128 : at + 256].astype(F32)
            t2 = both[:, at + 256 : at + 384].astype(F32)
            odd = jnp.where(low, t2, t1).astype(BF16)
            pair = jnp.where(low, t1, t2)
            swapped = jnp.where(lane % 64 < 32, pltpu.roll(pair, 96, 1), pltpu.roll(pair, 32, 1))
            turned = pair * rope_s[:, :128] + swapped * rope_s[:, 128:]
            out[even, :, :KVR] = jnp.dot(t0, ka[even], preferred_element_type=F32).astype(BF16)
            odd_key = jnp.concatenate([ka[even + 1, 64:, :], ka[even + 1, :64, :]], axis=0)
            out[even + 1, :, :KVR] = jnp.dot(odd, odd_key, preferred_element_type=F32).astype(BF16)
            out[even, :, KVR:] = jnp.where(low, turned, ext_s[...]).astype(BF16)
            turned = pltpu.roll(turned, 64, 1)
            out[even + 1, :, KVR:] = jnp.where(low, turned, ext_s[...]).astype(BF16)
        heads = pl.ds(c * HEADS // chunks, HEADS // chunks)
        done = pltpu.make_async_copy(out.at[heads], out_h.at[heads], sem.at[4 + chunks + c])
        done.start()
        outgoing.append(done)
    for done in outgoing:
        done.wait()


HBM = pl.BlockSpec(memory_space=pltpu.HBM)
VMEM = pl.BlockSpec(memory_space=pltpu.VMEM)
TOKEN = jax.ShapeDtypeStruct((8, 128), F32)


def queries(blk, ql, qu, ka, follow, chunks=4):
    width = qu.shape[1] // chunks
    table = np.concatenate(rope_tables(), axis=0)
    return pl.pallas_call(
        query_kernel,
        in_specs=[HBM] * 6,
        out_specs=[HBM, VMEM],
        scratch_shapes=[
            pltpu.SMEM(blk.shape, jnp.int32),
            pltpu.VMEM(ql.shape, BF16),
            pltpu.VMEM((chunks, qu.shape[0], width), BF16),
            pltpu.VMEM(ka.shape, BF16),
            pltpu.VMEM(table.shape, F32),
            pltpu.VMEM((HEADS, ROWS, WIDE), BF16),
            pltpu.VMEM((ROWS, 256), F32),
            pltpu.VMEM((ROWS, 128), F32),
            pltpu.SemaphoreType.DMA((4 + 2 * chunks,)),
        ],
        out_shape=[jax.ShapeDtypeStruct((HEADS, ROWS, WIDE), BF16), TOKEN],
        compiler_params=pltpu.CompilerParams(vmem_limit_bytes=QUERY_VMEM),
        cost_estimate=pl.CostEstimate(
            flops=int(2.6e9), bytes_accessed=int(15e6), transcendentals=0
        ),
        name="queries",
    )(blk, ql, qu, ka, jnp.asarray(table), follow)


def join_kernel(count, groups, *refs):
    outs = refs[len(refs) - len(groups) :]
    for group, out in zip(groups, outs):
        at = 0
        for i in group:
            piece = refs[i]
            out[at : at + piece.shape[0], :] = piece[...]
            at += piece.shape[0]


def join(pieces, groups, *follow):
    rows = [sum(pieces[i].shape[0] for i in group) for group in groups]
    return pl.pallas_call(
        functools.partial(join_kernel, len(pieces), groups),
        in_specs=[VMEM] * len(pieces) + [HBM] * len(follow),
        out_specs=[VMEM] * len(groups),
        out_shape=[jax.ShapeDtypeStruct((n, WIDE), BF16) for n in rows],
        compiler_params=pltpu.CompilerParams(vmem_limit_bytes=SMALL_VMEM),
        cost_estimate=pl.CostEstimate(flops=0, bytes_accessed=10**6, transcendentals=0),
        name="join",
    )(*pieces, *follow)


def lanes(op, a):
    parts = [a[:, at : at + 128] for at in range(0, a.shape[1], 128)]
    while len(parts) > 1:
        pairs = [parts[i : i + 2] for i in range(0, len(parts), 2)]
        parts = [op(*pair) if len(pair) == 2 else pair[0] for pair in pairs]
    return parts[0]


def attend_kernel(sizes, group, first, last, follows, *refs):
    refs = list(refs)
    q_ref = refs.pop(0)
    pieces = [refs.pop(0) for _ in sizes]
    if follows:
        refs.pop(0)
    if not first:
        state_in = refs.pop(0)
    if last:
        up_ref, out_ref = refs.pop(0), refs.pop(0)
    else:
        state_out, token = refs.pop(0), refs.pop(0)
    keys = refs.pop(0)
    mask = refs.pop(0) if first else None
    pair = 2
    rows = pair * ROWS

    @pl.when(pl.program_id(0) == 0)
    def _():
        at = 0
        for size, piece in zip(sizes, pieces):
            keys[at : at + size, :] = piece[...]
            at += size
        if not last:
            token[...] = jnp.zeros(token.shape, F32)
        if first:
            r = lax.broadcasted_iota(jnp.int32, (ROWS, 256), 0)
            t = lax.broadcasted_iota(jnp.int32, (ROWS, 256), 1)
            same = ((r < HALF) & (t < HALF)) | ((r >= HALF) & (t >= HALF) & (t < ROWS))
            mask[...] = jnp.where(same & (t > r), -BIG, 0.0)

    def score(j):
        q = q_ref[j * pair : (j + 1) * pair].reshape(rows, WIDE)
        s = lax.dot_general(q, keys[...], (((1,), (1,)), ((), ())), preferred_element_type=F32)
        if first:
            head = (s[:, :256].reshape(pair, ROWS, 256) + mask[...]).reshape(rows, 256)
            s = jnp.concatenate([head, s[:, 256:]], axis=1)
        return s

    def finish(j, s):
        peak = jnp.max(lanes(jnp.maximum, s), axis=1, keepdims=True)
        here = slice(j * pair, (j + 1) * pair)
        if not first:
            marks = state_in[here, :, KVR:].reshape(rows, 128).astype(F32)
            old_peak = marks[:, 0:1] + marks[:, 1:2] + marks[:, 2:3]
            old_total = marks[:, 3:4] + marks[:, 4:5] + marks[:, 5:6]
            peak = jnp.maximum(peak, old_peak)
            shrink = jnp.exp2((old_peak - peak) * SCALE2)
        level = peak * SCALE2
        acc, total = None, None
        for at in range(0, s.shape[1], CHUNK):
            weights = jnp.exp2(s[:, at : at + CHUNK] * SCALE2 - level)
            part = lanes(jnp.add, weights)
            total = part if total is None else total + part
            part = jnp.dot(
                weights.astype(BF16), keys[at : at + CHUNK, :KVR], preferred_element_type=F32
            )
            acc = part if acc is None else acc + part
        total = jnp.sum(total, axis=1, keepdims=True)
        if not first:
            total = total + old_total * shrink
            acc = acc + state_in[here, :, :KVR].reshape(rows, KVR).astype(F32) * shrink
        if last:
            latent = (acc * (1.0 / total)).astype(BF16)
            for k in range(pair):
                h = j * pair + k
                out_ref[:, h * VD : (h + 1) * VD] = jnp.dot(
                    latent[k * ROWS : (k + 1) * ROWS], up_ref[h], preferred_element_type=F32
                ).astype(BF16)
        else:
            lane = lax.broadcasted_iota(jnp.int32, (rows, 128), 1)
            marks = jnp.zeros((rows, 128), F32)
            for base, rest in ((0, peak), (3, total)):
                for part in range(3):
                    top = rest.astype(BF16).astype(F32)
                    marks = jnp.where(lane == base + part, top, marks)
                    rest = rest - top
            state_out[here, :, KVR:] = marks.astype(BF16).reshape(pair, ROWS, 128)
            state_out[here, :, :KVR] = acc.astype(BF16).reshape(pair, ROWS, KVR)

    steps = group // pair
    s = score(0)
    for j in range(steps):
        after = score(j + 1) if j + 1 < steps else None
        finish(j, s)
        s = after


def attend(q, pieces, state=None, up=None, group=4, follow=None):
    pieces = [piece if isinstance(piece, tuple) else (piece, 0, piece.shape[0]) for piece in pieces]
    sizes = [size for _, _, size in pieces]
    first, last = state is None, up is not None
    span = sum(sizes)
    heads = lambda width: pl.BlockSpec((group, ROWS, width), lambda i: (i, 0, 0))
    in_specs = [heads(WIDE)] + [
        pl.BlockSpec((size, WIDE), lambda i, at=at: (at, 0)) for _, at, size in pieces
    ]
    args = [q, *(piece for piece, _, _ in pieces)]
    if follow is not None:
        in_specs.append(HBM)
        args.append(follow)
    if not first:
        in_specs.append(heads(WIDE))
        args.append(state)
    if last:
        in_specs.append(pl.BlockSpec((group, KVR, VD), lambda i: (i, 0, 0)))
        args.append(up)
        out_specs = pl.BlockSpec((ROWS, group * VD), lambda i: (0, i))
        out_shape = jax.ShapeDtypeStruct((ROWS, HEADS * VD), BF16)
    else:
        out_specs = [heads(WIDE), pl.BlockSpec((8, 128), lambda i: (0, 0))]
        out_shape = [
            jax.ShapeDtypeStruct((HEADS, ROWS, WIDE), BF16),
            TOKEN,
        ]
    scratch = [pltpu.VMEM((span, WIDE), BF16)]
    if first:
        scratch.append(pltpu.VMEM((ROWS, 256), F32))
    flops = 2 * HEADS * ROWS * span * (768 + KVR)
    return pl.pallas_call(
        functools.partial(attend_kernel, sizes, group, first, last, follow is not None),
        grid=(HEADS // group,),
        in_specs=in_specs,
        out_specs=out_specs,
        out_shape=out_shape,
        scratch_shapes=scratch,
        compiler_params=pltpu.CompilerParams(vmem_limit_bytes=ATTEND_VMEM),
        cost_estimate=pl.CostEstimate(
            flops=flops, bytes_accessed=int(16e6), transcendentals=HEADS * ROWS * span
        ),
        name="attend_first" if first else "attend_last" if last else "attend_next",
    )(*args)


def pack_kernel(blk_h, owners_h, kv_h, out, cut, blk, owners, kv, sem):
    copies = [
        pltpu.make_async_copy(blk_h, blk, sem.at[0]),
        pltpu.make_async_copy(owners_h, owners, sem.at[1]),
        pltpu.make_async_copy(kv_h, kv, sem.at[2]),
    ]
    for copy in copies:
        copy.start()
    cut[...] = jnp.zeros(cut.shape, BF16)
    row = lax.broadcasted_iota(jnp.int32, (ROWS, 128), 0)
    lane = lax.broadcasted_iota(jnp.int32, (ROWS, 128), 1)
    copies[0].wait()
    copies[1].wait()
    first = row < HALF
    marks = (lane == 64 + jnp.where(first, blk[0, 0], blk[0, 1])) | (
        lane == 64 + BLOCKS + jnp.where(first, row, row - HALF) // PAGE
    )
    copies[2].wait()
    out[:, :KVR] = kv[:, :KVR]
    tail = jnp.concatenate([kv[:, KVR:], jnp.zeros((ROWS, 64), BF16)], axis=1).astype(F32)
    out[:, KVR:] = jnp.where(marks, 1.0, tail).astype(BF16)
    for p in range(PAGES):
        owner = owners[0, p]
        rank = jnp.int32(0)
        for earlier in range(p):
            rank = rank + jnp.where(owners[0, earlier] == owner, 1, 0)
        at = pl.multiple_of((owner * CAP + rank) * PAGE, PAGE)
        cut[pl.ds(at, PAGE), :] = out[p * PAGE : (p + 1) * PAGE, :]


def pack(blk, owners, kv):
    return pl.pallas_call(
        pack_kernel,
        in_specs=[HBM, HBM, HBM],
        out_specs=[VMEM, VMEM],
        out_shape=[
            jax.ShapeDtypeStruct((ROWS, WIDE), BF16),
            jax.ShapeDtypeStruct((8 * CAP * PAGE, WIDE), BF16),
        ],
        scratch_shapes=[
            pltpu.SMEM(blk.shape, jnp.int32),
            pltpu.SMEM(owners.shape, jnp.int32),
            pltpu.VMEM(kv.shape, BF16),
            pltpu.SemaphoreType.DMA((3,)),
        ],
        compiler_params=pltpu.CompilerParams(vmem_limit_bytes=VMEM_LIMIT),
        cost_estimate=pl.CostEstimate(flops=10**5, bytes_accessed=10**6, transcendentals=0),
        name="pack",
    )(blk, owners, kv)


def place_kernel(got, _, out, start, wide):
    rows = CAP * PAGE
    for t in range(WIDE // 128):
        wide[t] = got[:, t * 128 : (t + 1) * 128].astype(F32)
    lane = lax.broadcasted_iota(jnp.int32, (8, 128), 1)
    eye = lax.broadcasted_iota(jnp.int32, (8, 128), 0) == lane
    is_block = (lane >= 64) & (lane < 64 + BLOCKS)
    is_page = (lane >= 64 + BLOCKS) & (lane < 70 + BLOCKS)
    place = jnp.where(is_block, (lane - 64) * HALF, (lane - 64 - BLOCKS) * PAGE).astype(F32)
    place = jnp.where(is_block | is_page, place, 0.0)
    for k in range(CAP):
        for r in range(0, PAGE, 2):
            pair = []
            for i in range(2):
                every = pl.ds(k * PAGE + r + i, 8, stride=rows)
                parts = [wide[t, every, :] for t in range(WIDE // 128)]
                pair.append(jnp.concatenate(parts, axis=1))
            if r == 0:
                mark = pair[0][:, KVR:]
                where = jnp.sum(mark * place, axis=1, keepdims=True)
                there = jnp.sum(jnp.where(is_block, mark, 0.0), axis=1, keepdims=True)
                where = jnp.where(there > 0.5, where, -1.0)
                where = jnp.sum(jnp.where(eye, where, 0.0), axis=0, keepdims=True)
                start[k] = where[:, :8].astype(jnp.int32)
            both = jnp.concatenate([pair[0][:, :LAT], pair[1][:, :LAT]], axis=1)
            out[k, :, r * LAT : (r + 2) * LAT] = both.astype(BF16)


def place_pages(got, follow):
    return pl.pallas_call(
        place_kernel,
        in_specs=[VMEM, HBM],
        out_specs=[VMEM, VMEM],
        out_shape=[
            jax.ShapeDtypeStruct((CAP, 8, FLAT), BF16),
            jax.ShapeDtypeStruct((CAP, 1, 8), jnp.int32),
        ],
        scratch_shapes=[pltpu.VMEM((WIDE // 128, got.shape[0], 128), F32)],
        compiler_params=pltpu.CompilerParams(vmem_limit_bytes=SMALL_VMEM),
        cost_estimate=pl.CostEstimate(flops=10**7, bytes_accessed=10**6, transcendentals=0),
        name="place_pages",
    )(got, follow)


def along_ctx(a, core0, core1=None):
    pairs = []
    for i in range(16):
        x, y, c = i // 4, i // 2 % 2, i % 2
        dx, dy, dc = core1 if c and core1 else core0
        pairs.append((i, (x + dx) % 4 * 4 + (y + dy) % 2 * 2 + (c + dc) % 2))
    return lax.ppermute(a, "ctx", pairs)


def per_device(ql, kv, qu, ka, vu, block_order, page_owner):
    ql, kv = ql[0], kv[0]
    own, cut = pack(block_order, page_owner[:, :, 0], kv)
    sibling = (0, 0, 1)
    y = along_ctx(own, (0, 1, 0))
    xp = along_ctx(own, (1, 0, 0))
    xm = along_ctx(own, (3, 0, 0))
    got = lax.all_to_all(cut.reshape(8, CAP * PAGE, WIDE), "prompt", 0, 0, tiled=True)
    got = got.reshape(8 * CAP * PAGE, WIDE)
    q, token = queries(block_order, ql, qu, ka, own)
    both, near = join([own, y, xp, xm], ((0, 1), (0, 1, 2, 3)), token)
    near_s = along_ctx(near, sibling)
    yxp = along_ctx(y, (1, 0, 0))
    yxm = along_ctx(y, (3, 0, 0))
    two = along_ctx(both, (2, 0, 0))
    state, token = attend(q, [near, near_s], group=8)
    (far,) = join([yxp, yxm, two], ((0, 1, 2),), token, got)
    far_s = along_ctx(far, sibling)
    cache, start = place_pages(got, token)
    out = attend(q, [far, far_s], state, vu, group=8)

    cache = jnp.transpose(cache, (1, 0, 2))[None, None]
    start = jnp.transpose(start, (1, 2, 0))[None]
    return out[None], cache, start


def solution(mesh):
    return jax.shard_map(
        per_device,
        mesh=mesh,
        in_specs=(
            P("prompt", "ctx", None),
            P("prompt", "ctx", None),
            P(),
            P(),
            P(),
            P("prompt", "ctx"),
            P("prompt", "ctx", None),
        ),
        out_specs=(
            P("prompt", "ctx", None),
            P("prompt", "ctx", None, None, None),
            P("prompt", "ctx", None, None),
        ),
        check_vma=False,
    )
```

profile of v0, /device:TPU:0, one launch (start us, length us, event | category | flops | bytes accessed | tf_op | source)
XLA Modules:
  0.0 67.1 jit_solution(16016764314320519838)
XLA Ops:
  0.6 1.9 %pack.1 = (bf16[192,640]{1,0:T(8,128)(2,1)}, bf16[384,640]{1,0:T(8,128)(2,1)}) custom-call(s32[1,2]{1,0:T(1,128)} %blk_h.3, s32[1,12]{1,0:T(1,128)} %bitcast.18, bf16[192,576]{1,0:T(8,128)(2,1)} %bitcast.17), custom_call_target="tpu_custom_call" | custom-call | flops 100000 | bytes 1000000 | tf_op jit(solution)/shard_map/pack/pallas_call | solution.py:332
  2.6 3.4 %collective-permute-start = (bf16[192,640]{1,0:T(8,128)(2,1)}, bf16[192,640]{1,0:T(8,128)(2,1)S(1)}, u32[]{:S(2)}, u32[]{:S(2)}) collective-permute-start(bf16[192,640]{1,0:T(8,128)(2,1)} %get-tuple-element.13._.refs_0_), channel_id=1, source_target_pairs={{0,2},{1,3},{2,0},{3,1},{4,6},{5,7},{6,4},{7,5},{8,10},{9,11},{10,... | collective-permute-start | bytes 737288 | tf_op jit(solution)/shard_map/ppermute | solution.py:402
  5.9 1.5 %collective-permute-start.3 = (bf16[192,640]{1,0:T(8,128)(2,1)}, bf16[192,640]{1,0:T(8,128)(2,1)S(1)}, u32[]{:S(2)}, u32[]{:S(2)}) collective-permute-start(bf16[192,640]{1,0:T(8,128)(2,1)} %get-tuple-element.13._.refs_0_), channel_id=1, source_target_pairs={{0,4},{1,5},{2,6},{3,7},{4,8},{5,9},{6,10},{7,11},{8,12},{9,13},{1... | collective-permute-start | bytes 737288 | tf_op jit(solution)/shard_map/ppermute | solution.py:402
  7.4 1.7 %collective-permute-start.4 = (bf16[192,640]{1,0:T(8,128)(2,1)}, bf16[192,640]{1,0:T(8,128)(2,1)S(1)}, u32[]{:S(2)}, u32[]{:S(2)}) collective-permute-start(bf16[192,640]{1,0:T(8,128)(2,1)} %get-tuple-element.13._.refs_0_), channel_id=1, source_target_pairs={{0,12},{1,13},{2,14},{3,15},{4,0},{5,1},{6,2},{7,3},{8,4},{9,5},{1... | collective-permute-start | bytes 737288 | tf_op jit(solution)/shard_map/ppermute | solution.py:402
  9.2 0.0 copy-start
  9.2 7.8 %queries.1 = (bf16[16,192,640]{2,1,0:T(8,128)(2,1)}, f32[8,128]{1,0:T(8,128)}) custom-call(s32[1,2]{1,0:T(1,128)} %blk_h.3, bf16[192,1536]{1,0:T(8,128)(2,1)} %bitcast.16, bf16[1536,3072]{1,0:T(8,128)(2,1)} %qu_h.1, bf16[16,128,512]{2,1,0:T(8,128)(2,1)} %ka_h.1, f32[128,256]{1,0:T(8,128)} %constant.2.clone.tab_h, bf16[192,640]{1,0:T(8,128)(2,1)} %get-tuple-element.13._.refs_0_), custom_call_target="tpu_custom_call" | custom-call | flops 2600000000 | bytes 15000000 | tf_op jit(solution)/shard_map/queries/pallas_call | solution.py:112
  17.0 0.0 collective-permute-done.refs_1_
  17.0 0.0 collective-permute-done.3.refs_2_
  17.0 0.0 collective-permute-done.4.refs_3_
  17.0 0.0 copy-done
  17.0 0.0 copy-start.1
  17.0 0.7 copy-done.1
  17.7 0.1 join.2
  17.8 0.1 collective-permute-start.6
  17.9 5.4 %all-to-all-start = ((bf16[8,48,640]{2,1,0:T(8,128)(2,1)}), bf16[8,48,640]{2,1,0:T(8,128)(2,1)S(1)}, u32[]{:S(2)}, u32[]{:S(2)}) async-start(bf16[8,48,640]{2,1,0:T(8,128)(2,1)} %bitcast.3), calls=%async_computation | async-start | bytes 983040 | tf_op jit(solution)/shard_map/all_to_all | solution.py:412
  23.4 1.8 %collective-permute-start.5 = (bf16[384,640]{1,0:T(8,128)(2,1)S(1)}, bf16[384,640]{1,0:T(8,128)(2,1)S(1)}, u32[]{:S(2)}, u32[]{:S(2)}) collective-permute-start(bf16[384,640]{1,0:T(8,128)(2,1)S(1)} %get-tuple-element.16), channel_id=1, source_target_pairs={{0,8},{1,9},{2,10},{3,11},{4,12},{5,13},{6,14},{7,15},{8,0},{9,1},... | collective-permute-start | bytes 1474568 | tf_op jit(solution)/shard_map/ppermute | solution.py:402
  25.2 0.6 collective-permute-start.1
  25.8 2.6 %collective-permute-start.2 = (bf16[192,640]{1,0:T(8,128)(2,1)S(1)}, bf16[192,640]{1,0:T(8,128)(2,1)S(1)}, u32[]{:S(2)}, u32[]{:S(2)}) collective-permute-start(bf16[192,640]{1,0:T(8,128)(2,1)S(1)} %collective-permute-done.refs_1_), channel_id=1, source_target_pairs={{0,12},{1,13},{2,14},{3,15},{4,0},{5,1},{6,2},{7,3},{8,4},{9,5},{1... | collective-permute-start | bytes 737288 | tf_op jit(solution)/shard_map/ppermute | solution.py:402
  28.4 0.0 collective-permute-done.6.refs_2_
  28.4 17.5 %attend_first.1 = (bf16[16,192,640]{2,1,0:T(8,128)(2,1)}, f32[8,128]{1,0:T(8,128)S(1)}) custom-call(bf16[16,192,640]{2,1,0:T(8,128)(2,1)} %get-tuple-element.14.refs_0_, bf16[768,640]{1,0:T(8,128)(2,1)S(1)} %get-tuple-element.17.refs_1_, bf16[768,640]{1,0:T(8,128)(2,1)} %collective-permute-done.6.refs_2_), custom_call_target="tpu_custom_call" | custom-call | flops 12079595520 | bytes 16000000 | tf_op jit(solution)/shard_map/attend_first/pallas_call | solution.py:286
  46.0 0.0 all-to-all-done
  46.0 0.0 collective-permute-done.1.refs_0_
  46.0 0.0 collective-permute-done.2.refs_1_
  46.0 0.0 collective-permute-done.5.refs_2_
  46.0 0.1 join.3.refs_1_
  46.1 0.3 collective-permute-start.7
  46.4 1.2 %place_pages.1 = (bf16[3,8,9216]{2,1,0:T(8,128)(2,1)}, s32[3,1,8]{2,1,0:T(1,128)}) custom-call(bf16[384,640]{1,0:T(8,128)(2,1)S(1)} %bitcast.15, f32[8,128]{1,0:T(8,128)S(1)} %get-tuple-element.18.refs_3_._), custom_call_target="tpu_custom_call" | custom-call | flops 10000000 | bytes 1000000 | tf_op jit(solution)/shard_map/place_pages/pallas_call | solution.py:381
  47.6 1.4 %collective-permute-done.7.refs_2_ = bf16[768,640]{1,0:T(8,128)(2,1)S(1)} collective-permute-done((bf16[768,640]{1,0:T(8,128)(2,1)S(1)}, bf16[768,640]{1,0:T(8,128)(2,1)S(1)}, u32[]{:S(2)}, u32[]{:S(2)}) %collective-permute-start.7) | collective-permute-done | bytes 983072 | tf_op jit(solution)/shard_map/ppermute | solution.py:402
  48.9 18.2 %attend_last.1 = bf16[192,2048]{1,0:T(8,128)(2,1)} custom-call(bf16[16,192,640]{2,1,0:T(8,128)(2,1)} %get-tuple-element.14.refs_0_, bf16[768,640]{1,0:T(8,128)(2,1)S(1)} %join.3.refs_1_, bf16[768,640]{1,0:T(8,128)(2,1)S(1)} %collective-permute-done.7.refs_2_, bf16[16,192,640]{2,1,0:T(8,128)(2,1)} %get-tuple-element.20.refs_3_, bf16[16,512,128]{2,1,0:T(8,128)(2,1)} %refs_4_.1), custom_call_target="tpu_custom_call" | custom-call | flops 12079595520 | bytes 16000000 | tf_op jit(solution)/shard_map/attend_last/pallas_call | solution.py:286
Async XLA Ops:
  2.6 14.4 %collective-permute-start = (bf16[192,640]{1,0:T(8,128)(2,1)}, bf16[192,640]{1,0:T(8,128)(2,1)S(1)}, u32[]{:S(2)}, u32[]{:S(2)}) collective-permute-start(bf16[192,640]{1,0:T(8,128)(2,1)} %get-tuple-element.13._.refs_0_), channel_id=1, source_target_pairs={{0,2},{1,3},{2,0},{3,1},{4,6},{5,7},{6,4},{7,5},{8,10},{9,11},{10,... | collective-permute-start | bytes 737288 | tf_op jit(solution)/shard_map/ppermute | solution.py:402
  5.9 11.1 %collective-permute-start.3 = (bf16[192,640]{1,0:T(8,128)(2,1)}, bf16[192,640]{1,0:T(8,128)(2,1)S(1)}, u32[]{:S(2)}, u32[]{:S(2)}) collective-permute-start(bf16[192,640]{1,0:T(8,128)(2,1)} %get-tuple-element.13._.refs_0_), channel_id=1, source_target_pairs={{0,4},{1,5},{2,6},{3,7},{4,8},{5,9},{6,10},{7,11},{8,12},{9,13},{1... | collective-permute-start | bytes 737288 | tf_op jit(solution)/shard_map/ppermute | solution.py:402
  7.4 9.6 %collective-permute-start.4 = (bf16[192,640]{1,0:T(8,128)(2,1)}, bf16[192,640]{1,0:T(8,128)(2,1)S(1)}, u32[]{:S(2)}, u32[]{:S(2)}) collective-permute-start(bf16[192,640]{1,0:T(8,128)(2,1)} %get-tuple-element.13._.refs_0_), channel_id=1, source_target_pairs={{0,12},{1,13},{2,14},{3,15},{4,0},{5,1},{6,2},{7,3},{8,4},{9,5},{1... | collective-permute-start | bytes 737288 | tf_op jit(solution)/shard_map/ppermute | solution.py:402
  9.2 7.9 %copy-start = (bf16[192,640]{1,0:T(8,128)(2,1)S(1)}, bf16[192,640]{1,0:T(8,128)(2,1)}, u32[]{:S(2)}) copy-start(bf16[192,640]{1,0:T(8,128)(2,1)} %get-tuple-element.13._.refs_0_) | copy-start | bytes 737284
  17.0 0.7 %copy-start.1 = (f32[8,128]{1,0:T(8,128)S(1)}, f32[8,128]{1,0:T(8,128)}, u32[]{:S(2)}) copy-start(f32[8,128]{1,0:T(8,128)} %get-tuple-element.15.refs_4_) | copy-start | bytes 12292
  17.8 10.6 %collective-permute-start.6 = (bf16[768,640]{1,0:T(8,128)(2,1)S(1)}, bf16[768,640]{1,0:T(8,128)(2,1)}, u32[]{:S(2)}, u32[]{:S(2)}) collective-permute-start(bf16[768,640]{1,0:T(8,128)(2,1)S(1)} %get-tuple-element.17.refs_1_), channel_id=1, source_target_pairs={{0,1},{1,0},{2,3},{3,2},{4,5},{5,4},{6,7},{7,6},{8,9},{9,8},{10,11... | collective-permute-start | bytes 2949128 | tf_op jit(solution)/shard_map/ppermute | solution.py:402
  17.9 28.0 %all-to-all-start = ((bf16[8,48,640]{2,1,0:T(8,128)(2,1)}), bf16[8,48,640]{2,1,0:T(8,128)(2,1)S(1)}, u32[]{:S(2)}, u32[]{:S(2)}) async-start(bf16[8,48,640]{2,1,0:T(8,128)(2,1)} %bitcast.3), calls=%async_computation | async-start | bytes 983040 | tf_op jit(solution)/shard_map/all_to_all | solution.py:412
  23.4 22.6 %collective-permute-start.5 = (bf16[384,640]{1,0:T(8,128)(2,1)S(1)}, bf16[384,640]{1,0:T(8,128)(2,1)S(1)}, u32[]{:S(2)}, u32[]{:S(2)}) collective-permute-start(bf16[384,640]{1,0:T(8,128)(2,1)S(1)} %get-tuple-element.16), channel_id=1, source_target_pairs={{0,8},{1,9},{2,10},{3,11},{4,12},{5,13},{6,14},{7,15},{8,0},{9,1},... | collective-permute-start | bytes 1474568 | tf_op jit(solution)/shard_map/ppermute | solution.py:402
  25.2 20.8 %collective-permute-start.1 = (bf16[192,640]{1,0:T(8,128)(2,1)S(1)}, bf16[192,640]{1,0:T(8,128)(2,1)S(1)}, u32[]{:S(2)}, u32[]{:S(2)}) collective-permute-start(bf16[192,640]{1,0:T(8,128)(2,1)S(1)} %collective-permute-done.refs_1_), channel_id=1, source_target_pairs={{0,4},{1,5},{2,6},{3,7},{4,8},{5,9},{6,10},{7,11},{8,12},{9,13},{1... | collective-permute-start | bytes 737288 | tf_op jit(solution)/shard_map/ppermute | solution.py:402
  25.8 20.2 %collective-permute-start.2 = (bf16[192,640]{1,0:T(8,128)(2,1)S(1)}, bf16[192,640]{1,0:T(8,128)(2,1)S(1)}, u32[]{:S(2)}, u32[]{:S(2)}) collective-permute-start(bf16[192,640]{1,0:T(8,128)(2,1)S(1)} %collective-permute-done.refs_1_), channel_id=1, source_target_pairs={{0,12},{1,13},{2,14},{3,15},{4,0},{5,1},{6,2},{7,3},{8,4},{9,5},{1... | collective-permute-start | bytes 737288 | tf_op jit(solution)/shard_map/ppermute | solution.py:402
  46.1 2.9 %collective-permute-start.7 = (bf16[768,640]{1,0:T(8,128)(2,1)S(1)}, bf16[768,640]{1,0:T(8,128)(2,1)S(1)}, u32[]{:S(2)}, u32[]{:S(2)}) collective-permute-start(bf16[768,640]{1,0:T(8,128)(2,1)S(1)} %join.3.refs_1_), channel_id=1, source_target_pairs={{0,1},{1,0},{2,3},{3,2},{4,5},{5,4},{6,7},{7,6},{8,9},{9,8},{10,11... | collective-permute-start | bytes 2949128 | tf_op jit(solution)/shard_map/ppermute | solution.py:402
where the time goes:
time: 68.4 us; the launch traced here: 67.1 us
  Pallas kernels  46.8 us (68%)
  starting transfers between devices  17.5 us (26%)
  waiting for transfers between devices  1.41 us (2%)
  between operations  0.74 us (1%)
    pallas_call x2, Pallas kernels, attend(): pl.pallas_call(functools.partial(attend_kernel, sizes, group, first, last...  35.7 us
    ppermute x8, starting transfers between devices, along_ctx(): return lax.ppermute(a, 'ctx', pairs)  12 us
    pallas_call x1, Pallas kernels, queries(): pl.pallas_call(query_kernel, in_specs=[HBM] * 6, out_specs=[HBM, VMEM], s...  7.82 us
    all_to_all x1, starting transfers between devices, per_device(): lax.all_to_all(cut.reshape(8, CAP * PAGE, WIDE), 'prompt', 0, 0, tiled=True)  5.44 us
    pallas_call x1, Pallas kernels, pack(): pl.pallas_call(pack_kernel, in_specs=[HBM, HBM, HBM], out_specs=[VMEM, VM...  1.93 us
    ppermute x8, waiting for transfers between devices, along_ctx(): return lax.ppermute(a, 'ctx', pairs)  1.41 us
  transfers between devices with their start and end apart: 9, of which 1 were waited for; matrix products, arithmetic and copies ran while one was open for 0% of the time, Pallas kernels for 40%

commit v1 on v0

--- a/solution.py
+++ b/solution.py
@@ -393,33 +393,31 @@
     )(got, follow)
 
 
-def along_ctx(a, core0, core1=None):
+def along_ctx(a, dx=0, dy=0, dc=0, flip=0):
     pairs = []
     for i in range(16):
         x, y, c = i // 4, i // 2 % 2, i % 2
-        dx, dy, dc = core1 if c and core1 else core0
-        pairs.append((i, (x + dx) % 4 * 4 + (y + dy) % 2 * 2 + (c + dc) % 2))
+        pairs.append((i, ((x ^ flip) + dx) % 4 * 4 + (y + dy) % 2 * 2 + (c + dc) % 2))
     return lax.ppermute(a, "ctx", pairs)
 
 
 def per_device(ql, kv, qu, ka, vu, block_order, page_owner):
     ql, kv = ql[0], kv[0]
     own, cut = pack(block_order, page_owner[:, :, 0], kv)
-    sibling = (0, 0, 1)
-    y = along_ctx(own, (0, 1, 0))
-    xp = along_ctx(own, (1, 0, 0))
-    xm = along_ctx(own, (3, 0, 0))
+    y = along_ctx(own, dy=1)
+    xp = along_ctx(own, dx=1)
+    xm = along_ctx(own, dx=3)
     got = lax.all_to_all(cut.reshape(8, CAP * PAGE, WIDE), "prompt", 0, 0, tiled=True)
     got = got.reshape(8 * CAP * PAGE, WIDE)
     q, token = queries(block_order, ql, qu, ka, own)
     both, near = join([own, y, xp, xm], ((0, 1), (0, 1, 2, 3)), token)
-    near_s = along_ctx(near, sibling)
-    yxp = along_ctx(y, (1, 0, 0))
-    yxm = along_ctx(y, (3, 0, 0))
-    two = along_ctx(both, (2, 0, 0))
+    near_s = along_ctx(near, dc=1)
+    yx1 = along_ctx(y, flip=1)
+    yx3 = along_ctx(y, flip=3)
+    two = along_ctx(both, flip=2)
     state, token = attend(q, [near, near_s], group=8)
-    (far,) = join([yxp, yxm, two], ((0, 1, 2),), token, got)
-    far_s = along_ctx(far, sibling)
+    (far,) = join([yx1, yx3, two], ((0, 1, 2),), token, got)
+    far_s = along_ctx(far, dc=1)
     cache, start = place_pages(got, token)
     out = attend(q, [far, far_s], state, vu, group=8)
 

time: 68.4 us -> 67.4 us (0.985)
  starting transfers between devices: 17.5 us -> 16.5 us
    ppermute x8, starting transfers between devices: 12 us -> 11.1 us  [along_ctx(): return lax.ppermute(a, 'ctx', pairs)]
where the time goes in v1:
time: 67.4 us; the launch traced here: 66.1 us
  Pallas kernels  46.8 us (69%)
  starting transfers between devices  16.5 us (24%)
  waiting for transfers between devices  1.41 us (2%)
  between operations  0.74 us (1%)
    pallas_call x2, Pallas kernels, attend(): pl.pallas_call(functools.partial(attend_kernel, sizes, group, first, last...  35.7 us
    ppermute x8, starting transfers between devices, along_ctx(): return lax.ppermute(a, 'ctx', pairs)  11.1 us
    pallas_call x1, Pallas kernels, queries(): pl.pallas_call(query_kernel, in_specs=[HBM] * 6, out_specs=[HBM, VMEM], s...  7.82 us
    all_to_all x1, starting transfers between devices, per_device(): lax.all_to_all(cut.reshape(8, CAP * PAGE, WIDE), 'prompt', 0, 0, tiled=True)  5.44 us
    pallas_call x1, Pallas kernels, pack(): pl.pallas_call(pack_kernel, in_specs=[HBM, HBM, HBM], out_specs=[VMEM, VM...  1.93 us
    ppermute x8, waiting for transfers between devices, along_ctx(): return lax.ppermute(a, 'ctx', pairs)  1.41 us
  transfers between devices with their start and end apart: 9, of which 1 were waited for; matrix products, arithmetic and copies ran while one was open for 0% of the time, Pallas kernels for 40%

profile of v1, /device:TPU:0, one launch (start us, length us, event | category | flops | bytes accessed | tf_op | source)
XLA Modules:
  0.0 66.1 jit_solution(3177259511904638936)
XLA Ops:
  0.6 1.9 %pack.1 = (bf16[192,640]{1,0:T(8,128)(2,1)}, bf16[384,640]{1,0:T(8,128)(2,1)}) custom-call(s32[1,2]{1,0:T(1,128)} %blk_h.3, s32[1,12]{1,0:T(1,128)} %bitcast.18, bf16[192,576]{1,0:T(8,128)(2,1)} %bitcast.17), custom_call_target="tpu_custom_call" | custom-call | flops 100000 | bytes 1000000 | tf_op jit(solution)/shard_map/pack/pallas_call | solution.py:332
  2.6 3.4 %collective-permute-start = (bf16[192,640]{1,0:T(8,128)(2,1)}, bf16[192,640]{1,0:T(8,128)(2,1)S(1)}, u32[]{:S(2)}, u32[]{:S(2)}) collective-permute-start(bf16[192,640]{1,0:T(8,128)(2,1)} %get-tuple-element.13._.refs_0_), channel_id=1, source_target_pairs={{0,2},{1,3},{2,0},{3,1},{4,6},{5,7},{6,4},{7,5},{8,10},{9,11},{10,... | collective-permute-start | bytes 737288 | tf_op jit(solution)/shard_map/ppermute | solution.py:401
  5.9 1.5 %collective-permute-start.3 = (bf16[192,640]{1,0:T(8,128)(2,1)}, bf16[192,640]{1,0:T(8,128)(2,1)S(1)}, u32[]{:S(2)}, u32[]{:S(2)}) collective-permute-start(bf16[192,640]{1,0:T(8,128)(2,1)} %get-tuple-element.13._.refs_0_), channel_id=1, source_target_pairs={{0,4},{1,5},{2,6},{3,7},{4,8},{5,9},{6,10},{7,11},{8,12},{9,13},{1... | collective-permute-start | bytes 737288 | tf_op jit(solution)/shard_map/ppermute | solution.py:401
  7.4 1.7 %collective-permute-start.4 = (bf16[192,640]{1,0:T(8,128)(2,1)}, bf16[192,640]{1,0:T(8,128)(2,1)S(1)}, u32[]{:S(2)}, u32[]{:S(2)}) collective-permute-start(bf16[192,640]{1,0:T(8,128)(2,1)} %get-tuple-element.13._.refs_0_), channel_id=1, source_target_pairs={{0,12},{1,13},{2,14},{3,15},{4,0},{5,1},{6,2},{7,3},{8,4},{9,5},{1... | collective-permute-start | bytes 737288 | tf_op jit(solution)/shard_map/ppermute | solution.py:401
  9.2 0.0 copy-start
  9.2 7.8 %queries.1 = (bf16[16,192,640]{2,1,0:T(8,128)(2,1)}, f32[8,128]{1,0:T(8,128)}) custom-call(s32[1,2]{1,0:T(1,128)} %blk_h.3, bf16[192,1536]{1,0:T(8,128)(2,1)} %bitcast.16, bf16[1536,3072]{1,0:T(8,128)(2,1)} %qu_h.1, bf16[16,128,512]{2,1,0:T(8,128)(2,1)} %ka_h.1, f32[128,256]{1,0:T(8,128)} %constant.2.clone.tab_h, bf16[192,640]{1,0:T(8,128)(2,1)} %get-tuple-element.13._.refs_0_), custom_call_target="tpu_custom_call" | custom-call | flops 2600000000 | bytes 15000000 | tf_op jit(solution)/shard_map/queries/pallas_call | solution.py:112
  17.0 0.0 collective-permute-done.refs_1_
  17.0 0.0 collective-permute-done.3.refs_2_
  17.0 0.0 collective-permute-done.4.refs_3_
  17.0 0.0 copy-done
  17.0 0.0 copy-start.1
  17.0 0.7 %copy-done.1 = f32[8,128]{1,0:T(8,128)S(1)} copy-done((f32[8,128]{1,0:T(8,128)S(1)}, f32[8,128]{1,0:T(8,128)}, u32[]{:S(2)}) %copy-start.1) | copy-done | bytes 4120
  17.7 0.1 join.2
  17.8 0.1 collective-permute-start.6
  17.9 5.4 %all-to-all-start = ((bf16[8,48,640]{2,1,0:T(8,128)(2,1)}), bf16[8,48,640]{2,1,0:T(8,128)(2,1)S(1)}, u32[]{:S(2)}, u32[]{:S(2)}) async-start(bf16[8,48,640]{2,1,0:T(8,128)(2,1)} %bitcast.3), calls=%async_computation | async-start | bytes 983040 | tf_op jit(solution)/shard_map/all_to_all | solution.py:410
  23.4 1.8 %collective-permute-start.5 = (bf16[384,640]{1,0:T(8,128)(2,1)S(1)}, bf16[384,640]{1,0:T(8,128)(2,1)S(1)}, u32[]{:S(2)}, u32[]{:S(2)}) collective-permute-start(bf16[384,640]{1,0:T(8,128)(2,1)S(1)} %get-tuple-element.16), channel_id=1, source_target_pairs={{0,8},{1,9},{2,10},{3,11},{4,12},{5,13},{6,14},{7,15},{8,0},{9,1},... | collective-permute-start | bytes 1474568 | tf_op jit(solution)/shard_map/ppermute | solution.py:401
  25.2 0.6 collective-permute-start.1
  25.8 1.7 %collective-permute-start.2 = (bf16[192,640]{1,0:T(8,128)(2,1)S(1)}, bf16[192,640]{1,0:T(8,128)(2,1)S(1)}, u32[]{:S(2)}, u32[]{:S(2)}) collective-permute-start(bf16[192,640]{1,0:T(8,128)(2,1)S(1)} %collective-permute-done.refs_1_), channel_id=1, source_target_pairs={{0,12},{1,13},{2,14},{3,15},{4,8},{5,9},{6,10},{7,11},{8,4},{9,5},... | collective-permute-start | bytes 737288 | tf_op jit(solution)/shard_map/ppermute | solution.py:401
  27.5 0.0 collective-permute-done.6.refs_2_
  27.5 17.5 %attend_first.1 = (bf16[16,192,640]{2,1,0:T(8,128)(2,1)}, f32[8,128]{1,0:T(8,128)S(1)}) custom-call(bf16[16,192,640]{2,1,0:T(8,128)(2,1)} %get-tuple-element.14.refs_0_, bf16[768,640]{1,0:T(8,128)(2,1)S(1)} %get-tuple-element.17.refs_1_, bf16[768,640]{1,0:T(8,128)(2,1)} %collective-permute-done.6.refs_2_), custom_call_target="tpu_custom_call" | custom-call | flops 12079595520 | bytes 16000000 | tf_op jit(solution)/shard_map/attend_first/pallas_call | solution.py:286
  45.0 0.0 all-to-all-done
  45.0 0.0 collective-permute-done.1.refs_0_
  45.0 0.0 collective-permute-done.2.refs_1_
  45.0 0.0 collective-permute-done.5.refs_2_
  45.0 0.1 join.3.refs_1_
  45.1 0.3 collective-permute-start.7
  45.4 1.2 %place_pages.1 = (bf16[3,8,9216]{2,1,0:T(8,128)(2,1)}, s32[3,1,8]{2,1,0:T(1,128)}) custom-call(bf16[384,640]{1,0:T(8,128)(2,1)S(1)} %bitcast.15, f32[8,128]{1,0:T(8,128)S(1)} %get-tuple-element.18.refs_3_._), custom_call_target="tpu_custom_call" | custom-call | flops 10000000 | bytes 1000000 | tf_op jit(solution)/shard_map/place_pages/pallas_call | solution.py:381
  46.6 1.4 %collective-permute-done.7.refs_2_ = bf16[768,640]{1,0:T(8,128)(2,1)S(1)} collective-permute-done((bf16[768,640]{1,0:T(8,128)(2,1)S(1)}, bf16[768,640]{1,0:T(8,128)(2,1)S(1)}, u32[]{:S(2)}, u32[]{:S(2)}) %collective-permute-start.7) | collective-permute-done | bytes 983072 | tf_op jit(solution)/shard_map/ppermute | solution.py:401
  48.0 18.2 %attend_last.1 = bf16[192,2048]{1,0:T(8,128)(2,1)} custom-call(bf16[16,192,640]{2,1,0:T(8,128)(2,1)} %get-tuple-element.14.refs_0_, bf16[768,640]{1,0:T(8,128)(2,1)S(1)} %join.3.refs_1_, bf16[768,640]{1,0:T(8,128)(2,1)S(1)} %collective-permute-done.7.refs_2_, bf16[16,192,640]{2,1,0:T(8,128)(2,1)} %get-tuple-element.20.refs_3_, bf16[16,512,128]{2,1,0:T(8,128)(2,1)} %refs_4_.1), custom_call_target="tpu_custom_call" | custom-call | flops 12079595520 | bytes 16000000 | tf_op jit(solution)/shard_map/attend_last/pallas_call | solution.py:286
Async XLA Ops:
  2.6 14.4 %collective-permute-start = (bf16[192,640]{1,0:T(8,128)(2,1)}, bf16[192,640]{1,0:T(8,128)(2,1)S(1)}, u32[]{:S(2)}, u32[]{:S(2)}) collective-permute-start(bf16[192,640]{1,0:T(8,128)(2,1)} %get-tuple-element.13._.refs_0_), channel_id=1, source_target_pairs={{0,2},{1,3},{2,0},{3,1},{4,6},{5,7},{6,4},{7,5},{8,10},{9,11},{10,... | collective-permute-start | bytes 737288 | tf_op jit(solution)/shard_map/ppermute | solution.py:401
  5.9 11.1 %collective-permute-start.3 = (bf16[192,640]{1,0:T(8,128)(2,1)}, bf16[192,640]{1,0:T(8,128)(2,1)S(1)}, u32[]{:S(2)}, u32[]{:S(2)}) collective-permute-start(bf16[192,640]{1,0:T(8,128)(2,1)} %get-tuple-element.13._.refs_0_), channel_id=1, source_target_pairs={{0,4},{1,5},{2,6},{3,7},{4,8},{5,9},{6,10},{7,11},{8,12},{9,13},{1... | collective-permute-start | bytes 737288 | tf_op jit(solution)/shard_map/ppermute | solution.py:401
  7.4 9.6 %collective-permute-start.4 = (bf16[192,640]{1,0:T(8,128)(2,1)}, bf16[192,640]{1,0:T(8,128)(2,1)S(1)}, u32[]{:S(2)}, u32[]{:S(2)}) collective-permute-start(bf16[192,640]{1,0:T(8,128)(2,1)} %get-tuple-element.13._.refs_0_), channel_id=1, source_target_pairs={{0,12},{1,13},{2,14},{3,15},{4,0},{5,1},{6,2},{7,3},{8,4},{9,5},{1... | collective-permute-start | bytes 737288 | tf_op jit(solution)/shard_map/ppermute | solution.py:401
  9.2 7.9 %copy-start = (bf16[192,640]{1,0:T(8,128)(2,1)S(1)}, bf16[192,640]{1,0:T(8,128)(2,1)}, u32[]{:S(2)}) copy-start(bf16[192,640]{1,0:T(8,128)(2,1)} %get-tuple-element.13._.refs_0_) | copy-start | bytes 737284
  17.0 0.7 %copy-start.1 = (f32[8,128]{1,0:T(8,128)S(1)}, f32[8,128]{1,0:T(8,128)}, u32[]{:S(2)}) copy-start(f32[8,128]{1,0:T(8,128)} %get-tuple-element.15.refs_4_) | copy-start | bytes 12292
  17.8 9.6 %collective-permute-start.6 = (bf16[768,640]{1,0:T(8,128)(2,1)S(1)}, bf16[768,640]{1,0:T(8,128)(2,1)}, u32[]{:S(2)}, u32[]{:S(2)}) collective-permute-start(bf16[768,640]{1,0:T(8,128)(2,1)S(1)} %get-tuple-element.17.refs_1_), channel_id=1, source_target_pairs={{0,1},{1,0},{2,3},{3,2},{4,5},{5,4},{6,7},{7,6},{8,9},{9,8},{10,11... | collective-permute-start | bytes 2949128 | tf_op jit(solution)/shard_map/ppermute | solution.py:401
  17.9 27.1 %all-to-all-start = ((bf16[8,48,640]{2,1,0:T(8,128)(2,1)}), bf16[8,48,640]{2,1,0:T(8,128)(2,1)S(1)}, u32[]{:S(2)}, u32[]{:S(2)}) async-start(bf16[8,48,640]{2,1,0:T(8,128)(2,1)} %bitcast.3), calls=%async_computation | async-start | bytes 983040 | tf_op jit(solution)/shard_map/all_to_all | solution.py:410
  23.4 21.6 %collective-permute-start.5 = (bf16[384,640]{1,0:T(8,128)(2,1)S(1)}, bf16[384,640]{1,0:T(8,128)(2,1)S(1)}, u32[]{:S(2)}, u32[]{:S(2)}) collective-permute-start(bf16[384,640]{1,0:T(8,128)(2,1)S(1)} %get-tuple-element.16), channel_id=1, source_target_pairs={{0,8},{1,9},{2,10},{3,11},{4,12},{5,13},{6,14},{7,15},{8,0},{9,1},... | collective-permute-start | bytes 1474568 | tf_op jit(solution)/shard_map/ppermute | solution.py:401
  25.2 19.8 %collective-permute-start.1 = (bf16[192,640]{1,0:T(8,128)(2,1)S(1)}, bf16[192,640]{1,0:T(8,128)(2,1)S(1)}, u32[]{:S(2)}, u32[]{:S(2)}) collective-permute-start(bf16[192,640]{1,0:T(8,128)(2,1)S(1)} %collective-permute-done.refs_1_), channel_id=1, source_target_pairs={{0,4},{1,5},{2,6},{3,7},{4,0},{5,1},{6,2},{7,3},{8,12},{9,13},{10,... | collective-permute-start | bytes 737288 | tf_op jit(solution)/shard_map/ppermute | solution.py:401
  25.8 19.2 %collective-permute-start.2 = (bf16[192,640]{1,0:T(8,128)(2,1)S(1)}, bf16[192,640]{1,0:T(8,128)(2,1)S(1)}, u32[]{:S(2)}, u32[]{:S(2)}) collective-permute-start(bf16[192,640]{1,0:T(8,128)(2,1)S(1)} %collective-permute-done.refs_1_), channel_id=1, source_target_pairs={{0,12},{1,13},{2,14},{3,15},{4,8},{5,9},{6,10},{7,11},{8,4},{9,5},... | collective-permute-start | bytes 737288 | tf_op jit(solution)/shard_map/ppermute | solution.py:401
  45.1 2.9 %collective-permute-start.7 = (bf16[768,640]{1,0:T(8,128)(2,1)S(1)}, bf16[768,640]{1,0:T(8,128)(2,1)S(1)}, u32[]{:S(2)}, u32[]{:S(2)}) collective-permute-start(bf16[768,640]{1,0:T(8,128)(2,1)S(1)} %join.3.refs_1_), channel_id=1, source_target_pairs={{0,1},{1,0},{2,3},{3,2},{4,5},{5,4},{6,7},{7,6},{8,9},{9,8},{10,11... | collective-permute-start | bytes 2949128 | tf_op jit(solution)/shard_map/ppermute | solution.py:401
